TPU v7x, 32 devices: a whole 2x2x4 slice. The times are simulated.
32 devices in a mesh: rows: 8 (over z, y), cols: 4 (over x, core).
Axes of the slice: x: 2, y: 2, z: 4, core: 2. Of those that a mesh axis runs over, the one named last changes fastest.
Arguments:
- coupling: float32 [4096, 8192], P('rows', 'cols'), may hold values from 0.1 to 10, as said below
- source: float32 [4096, 256], P('rows'), may hold values from -150 to 150
- target: float32 [8192, 256], P('cols'), may hold values from -6 to 6
Outputs:
- log_coupling: float32 [4096, 8192], P('rows', 'cols')
Inputs may be any that keep to these rules, and one draw needn't show every extreme that they name: `coupling`: positive entries.
All inputs are finite; a program needn't handle non-finite values.
Results may differ from a plain program's by a relative error of at most 0.0003.
Values sent between devices are 32-bit elements; how exact they have to be, the bound alone decides.
A program may use at most 64 MiB of HBM per device.

v0:
```python
import math

import jax
import jax.numpy as jnp
from jax import lax
from jax.sharding import PartitionSpec as P

R = 256
SWEEPS = 3


def row_logsumexp(values):
    local_top = jnp.max(values, axis=1)
    top = lax.pmax(local_top, "cols")
    total = lax.psum(jnp.sum(jnp.exp(values - top[:, None]), axis=1), "cols")
    return jnp.log(total) + top


def col_logsumexp(values):
    local_top = jnp.max(values, axis=0)
    top = lax.pmax(local_top, "rows")
    total = lax.psum(jnp.sum(jnp.exp(values - top[None, :]), axis=0), "rows")
    return jnp.log(total) + top


def on_device(coupling, source, target):
    highest = lax.Precision.HIGHEST
    total_rows = coupling.shape[0] * lax.axis_size("rows")
    total_cols = coupling.shape[1] * lax.axis_size("cols")
    slab = jnp.dot(coupling, target, precision=highest, preferred_element_type=jnp.float32)
    summed = lax.psum(slab, "cols")
    local_factor = jnp.dot(source.T, summed, precision=highest, preferred_element_type=jnp.float32)
    factor = lax.psum(local_factor, "rows")
    factor = factor / math.sqrt(total_rows * total_cols)
    mapped = jnp.dot(source, factor, precision=highest, preferred_element_type=jnp.float32)
    logits = (
        lax.dot_general(
            mapped,
            target,
            (((1,), (1,)), ((), ())),
            precision=highest,
            preferred_element_type=jnp.float32,
        )
        / R
    )
    colpot = jnp.zeros((coupling.shape[1],), jnp.float32)
    rowpot = jnp.zeros((coupling.shape[0],), jnp.float32)
    for sweep in range(SWEEPS):
        rowpot = math.log(total_cols) - row_logsumexp(logits + colpot[None, :])
        colpot = math.log(total_rows) - col_logsumexp(logits + rowpot[:, None])
    return logits + rowpot[:, None] + colpot[None, :]


def solution(mesh):
    placed = (P("rows", "cols"), P("rows", None), P("cols", None))
    return jax.shard_map(
        on_device, mesh=mesh, in_specs=placed, out_specs=P("rows", "cols"), check_vma=False
    )
```

profile of v0, /device:TPU:0, one launch (start us, length us, event | category | flops | bytes accessed | tf_op | source)
XLA Modules:
  0.0 324.2 jit_solution(3515773492459650442)
XLA Ops:
  6.5 1.6 copy-done
  8.1 6.4 %fusion.5 = f32[512,256]{1,0:T(8,128)} fusion(f32[512,2048]{1,0:T(8,128)} %param.3, f32[2048,256]{1,0:T(8,128)S(1)} %copy-done), kind=kOutput, calls=%fused_computation.25 | convolution fusion | flops 3221225472 | bytes 6815744 | tf_op jit(solution)/shard_map/dot_general | solution.py:30
  14.6 0.0 all-reduce.5.cloned.1.call-start
  14.6 36.0 %all-reduce.3.cloned.1.call-done = f32[512,256]{1,0:T(8,128)} async-done(((f32[512,256]{1,0:T(8,128)}), f32[512,256]{1,0:T(8,128)}) %all-reduce.3.cloned.1.call-update) | async-done | bytes 524304 | tf_op jit(solution)/shard_map/psum | solution.py:31
  50.6 2.7 convolution_bitcast_fusion
  53.4 71.1 %all-reduce.5.cloned.1.call-done = f32[256,256]{0,1:T(8,128)} async-done(((f32[256,256]{0,1:T(8,128)}), f32[256,256]{0,1:T(8,128)}) %all-reduce.5.cloned.1.call-update) | async-done | bytes 262160 | tf_op jit(solution)/shard_map/psum | solution.py:33
  124.5 1.6 fusion
  126.1 8.5 %fusion.4 = (f32[512]{0:T(512)S(1)}, f32[512,2048]{1,0:T(8,128)}) fusion(f32[256,512]{1,0:T(8,128)S(1)} %fusion, f32[2048,256]{1,0:T(8,128)S(1)} %copy-done), kind=kOutput, calls=%fused_computation.24 | convolution fusion | flops 3223322112 | bytes 6817792 | tf_op jit(solution)/shard_map/dot_general | solution.py:37
  134.6 5.6 %pmax.42 = f32[512]{0:T(512)S(1)} all-reduce(f32[512]{0:T(512)S(1)} %get-tuple-element.5), channel_id=1, replica_groups=mesh['rows'=8,'cols'=4] {'cols'}, use_global_device_ids=true, to_apply=%region_3.0 | all-reduce | flops 512 | bytes 4096 | tf_op jit(solution)/shard_map/pmax | solution.py:14
  140.2 2.9 exponential_reduce_fusion.5
  143.1 6.6 %psum.58 = f32[512]{0:T(512)S(1)} all-reduce(f32[512]{0:T(512)S(1)} %exponential_reduce_fusion.5), channel_id=1, replica_groups=mesh['rows'=8,'cols'=4] {'cols'}, use_global_device_ids=true, to_apply=%region_5.0 | all-reduce | flops 512 | bytes 4096 | tf_op jit(solution)/shard_map/psum | solution.py:15
  149.7 2.5 add_reduce_fusion.3
  152.3 19.9 %pmax.43 = f32[2048]{0:T(1024)S(1)} all-reduce(f32[2048]{0:T(1024)S(1)} %add_reduce_fusion.3), channel_id=1, replica_groups=mesh['rows'=8,'cols'=4] {'rows'}, use_global_device_ids=true, to_apply=%region_7.0 | all-reduce | flops 2048 | bytes 16384 | tf_op jit(solution)/shard_map/pmax | solution.py:21
  172.2 3.0 exponential_reduce_fusion.4
  175.2 17.4 %psum.59 = f32[2048]{0:T(1024)S(1)} all-reduce(f32[2048]{0:T(1024)S(1)} %exponential_reduce_fusion.4), channel_id=1, replica_groups=mesh['rows'=8,'cols'=4] {'rows'}, use_global_device_ids=true, to_apply=%region_9.0 | all-reduce | flops 2048 | bytes 16384 | tf_op jit(solution)/shard_map/psum | solution.py:22
  192.6 2.5 add_reduce_fusion.2
  195.2 5.8 %pmax.44 = f32[512]{0:T(512)S(1)} all-reduce(f32[512]{0:T(512)S(1)} %add_reduce_fusion.2), channel_id=1, replica_groups=mesh['rows'=8,'cols'=4] {'cols'}, use_global_device_ids=true, to_apply=%region_11.0 | all-reduce | flops 512 | bytes 4096 | tf_op jit(solution)/shard_map/pmax | solution.py:14
  201.0 3.0 exponential_reduce_fusion.3
  204.0 6.2 %psum.60 = f32[512]{0:T(512)S(1)} all-reduce(f32[512]{0:T(512)S(1)} %exponential_reduce_fusion.3), channel_id=1, replica_groups=mesh['rows'=8,'cols'=4] {'cols'}, use_global_device_ids=true, to_apply=%region_13.0 | all-reduce | flops 512 | bytes 4096 | tf_op jit(solution)/shard_map/psum | solution.py:15
  210.3 2.5 add_reduce_fusion.1
  212.8 19.4 %pmax.45 = f32[2048]{0:T(1024)S(1)} all-reduce(f32[2048]{0:T(1024)S(1)} %add_reduce_fusion.1), channel_id=1, replica_groups=mesh['rows'=8,'cols'=4] {'rows'}, use_global_device_ids=true, to_apply=%region_15.0 | all-reduce | flops 2048 | bytes 16384 | tf_op jit(solution)/shard_map/pmax | solution.py:21
  232.2 3.0 exponential_reduce_fusion.2
  235.2 17.4 %psum.61 = f32[2048]{0:T(1024)S(1)} all-reduce(f32[2048]{0:T(1024)S(1)} %exponential_reduce_fusion.2), channel_id=1, replica_groups=mesh['rows'=8,'cols'=4] {'rows'}, use_global_device_ids=true, to_apply=%region_17.0 | all-reduce | flops 2048 | bytes 16384 | tf_op jit(solution)/shard_map/psum | solution.py:22
  252.6 2.5 add_reduce_fusion
  255.1 5.7 %pmax.46 = f32[512]{0:T(512)S(1)} all-reduce(f32[512]{0:T(512)S(1)} %add_reduce_fusion), channel_id=1, replica_groups=mesh['rows'=8,'cols'=4] {'cols'}, use_global_device_ids=true, to_apply=%region_19.0 | all-reduce | flops 512 | bytes 4096 | tf_op jit(solution)/shard_map/pmax | solution.py:14
  260.8 3.0 exponential_reduce_fusion.1
  263.8 6.6 %psum.62 = f32[512]{0:T(512)S(1)} all-reduce(f32[512]{0:T(512)S(1)} %exponential_reduce_fusion.1), channel_id=1, replica_groups=mesh['rows'=8,'cols'=4] {'cols'}, use_global_device_ids=true, to_apply=%region_21.0 | all-reduce | flops 512 | bytes 4096 | tf_op jit(solution)/shard_map/psum | solution.py:15
  270.4 2.5 add_reduce_fusion.4
  273.0 19.3 %pmax.47 = f32[2048]{0:T(1024)S(1)} all-reduce(f32[2048]{0:T(1024)S(1)} %add_reduce_fusion.4), channel_id=1, replica_groups=mesh['rows'=8,'cols'=4] {'rows'}, use_global_device_ids=true, to_apply=%region_23.0 | all-reduce | flops 2048 | bytes 16384 | tf_op jit(solution)/shard_map/pmax | solution.py:21
  292.3 2.9 exponential_reduce_fusion
  295.2 17.4 %psum.63 = f32[2048]{0:T(1024)S(1)} all-reduce(f32[2048]{0:T(1024)S(1)} %exponential_reduce_fusion), channel_id=1, replica_groups=mesh['rows'=8,'cols'=4] {'rows'}, use_global_device_ids=true, to_apply=%region_25.0 | all-reduce | flops 2048 | bytes 16384 | tf_op jit(solution)/shard_map/psum | solution.py:22
  312.7 4.6 %add_add_fusion = f32[512,2048]{1,0:T(8,128)} fusion(f32[512,2048]{1,0:T(8,128)} %get-tuple-element.6, f32[2048]{0:T(1024)S(1)} %add_subtract_fusion, f32[512]{0:T(512)S(1)} %add_subtract_fusion.3), kind=kLoop, calls=%fused_computation.10 | loop fusion | flops 2097152 | bytes 8398848 | tf_op jit(solution)/shard_map/add | solution.py:51
  (12 shorter events, 0.1 us)
Async XLA Ops:
  6.5 1.6 copy-start
  6.5 44.1 %copy-start.1 = (f32[512,256]{1,0:T(8,128)S(1)}, f32[512,256]{1,0:T(8,128)}, u32[]{:S(2)}) copy-start(f32[512,256]{1,0:T(8,128)} %param.4) | copy-start | bytes 1572868
  6.5 44.1 %all-reduce.3.cloned.1.call-start = ((), (), s32[]{:S(2)}) async-start(), calls=%async_computation | async-start | bytes 1048576 | tf_op jit(solution)/shard_map/psum | solution.py:31
  14.6 109.9 %all-reduce.5.cloned.1.call-start = ((), (), s32[]{:S(2)}) async-start(), calls=%async_computation.1 | async-start | bytes 524288 | tf_op jit(solution)/shard_map/psum | solution.py:33
Sparse Core Ops, SparseCore 0:
  14.7 35.8 all-reduce.2
  54.0 70.5 all-reduce.4
where the time goes:
time: 325 us; the launch traced here: 324 us
  blocking collectives  147 us (45%)
  waiting for transfers between devices  107 us (33%)
  other arithmetic  35.1 us (11%)
  matrix products  19.2 us (6%)
  between operations  13.5 us (4%)
    psum x1, waiting for transfers between devices, on_device(): factor = lax.psum(local_factor, 'rows')  71.1 us
    pmax x3, blocking collectives, col_logsumexp(): top = lax.pmax(local_top, 'rows')  58.7 us
    psum x3, blocking collectives, col_logsumexp(): total = lax.psum(jnp.sum(jnp.exp(values - top[None, :]), axis=0), 'rows')  52.3 us
    psum x1, waiting for transfers between devices, on_device(): summed = lax.psum(slab, 'cols')  36 us
    psum x3, blocking collectives, row_logsumexp(): total = lax.psum(jnp.sum(jnp.exp(values - top[:, None]), axis=1), 'cols')  19.5 us
    pmax x3, blocking collectives, row_logsumexp(): top = lax.pmax(local_top, 'cols')  17.1 us
    reduce_sum x3, other arithmetic, row_logsumexp(): total = lax.psum(jnp.sum(jnp.exp(values - top[:, None]), axis=1), 'cols')  8.88 us
    reduce_sum x3, other arithmetic, col_logsumexp(): total = lax.psum(jnp.sum(jnp.exp(values - top[None, :]), axis=0), 'rows')  8.87 us
  transfers between devices with their start and end apart: 2, of which 2 were waited for; matrix products, arithmetic and copies ran while one was open for 0% of the time, Pallas kernels for 0%

commit v1 on v0

v1 whole, which is shorter than its diff:
```python
import functools
import math

import jax
import jax.numpy as jnp
from jax import lax
from jax.experimental import pallas as pl
from jax.experimental.pallas import tpu as pltpu
from jax.sharding import PartitionSpec as P

R = 256
SWEEPS = 3
LANES = 128
SUB = 8
DEPTH = 512
WIDE = 256
MESH = pl.DeviceIdType.MESH
HIGHEST = lax.Precision.HIGHEST


def tree(op, values):
    while len(values) > 1:
        paired = [op(a, b) for a, b in zip(values[::2], values[1::2])]
        values = paired + values[len(paired) * 2 :]
    return values[0]


def split(x):
    high = x.astype(jnp.bfloat16)
    return high, (x - high.astype(jnp.float32)).astype(jnp.bfloat16)


def dot3(left, right, dims):
    (lh, ll), (rh, rl) = left, right
    dot = functools.partial(
        lax.dot_general, dimension_numbers=(dims, ((), ())), preferred_element_type=jnp.float32
    )
    return dot(lh, rh) + (dot(lh, rl) + dot(ll, rh))


def lse_fold(top, total, axis):
    peak = jnp.max(top, axis=axis, keepdims=True)
    return peak + jnp.log(jnp.sum(total * jnp.exp(top - peak), axis=axis, keepdims=True))


def lse_merge(parts):
    peak = tree(jnp.maximum, parts)
    return peak + jnp.log(tree(jnp.add, [jnp.exp(part - peak) for part in parts]))


def step_kernel(
    nr, nc, owners,
    coupling_hbm, source_hbm, target_hbm,
    logits_hbm, rowpot_out, colpot_out,
    coupling, source, target, high, low, logits, slab, factor_part, factor,
    from_cols, part, from_rows, piece,
    row_top, row_sum, col_top, col_sum,
    row_send, row_recv, col_send, col_recv,
    load_sems, logits_sem,
    a_send, a_recv, b_send, b_recv, c_send, c_recv, d_send, d_recv,
    rs_send, rs_recv, cs_send, cs_recv,
):
    rows, cols = logits.shape
    total_rows, total_cols = rows * nr, cols * nc
    mr, mc = lax.axis_index("rows"), lax.axis_index("cols")
    depths = cols // DEPTH
    tiles, chunks, blocks = cols // LANES, rows // LANES, LANES // SUB

    def span(at, size):
        return pl.ds(pl.multiple_of(at * size, size), size)

    def load_target(k):
        return pltpu.make_async_copy(
            target_hbm.at[span(k, DEPTH), :], target.at[span(k, DEPTH), :], load_sems.at[0, k]
        )

    def load_coupling(k):
        return pltpu.make_async_copy(
            coupling_hbm.at[:, span(k, DEPTH)], coupling.at[:, span(k, DEPTH)], load_sems.at[1, k]
        )

    load_source = pltpu.make_async_copy(source_hbm, source, load_sems.at[0, depths])
    for k in range(depths):
        load_target(k).start()
        load_coupling(k).start()
    load_source.start()

    def on_rows(d):
        return lax.rem(mr + d, nr)

    def on_cols(d):
        return lax.rem(mc + d, nc)

    barrier = pltpu.get_barrier_semaphore()
    for d in range(1, nc):
        pl.semaphore_signal(barrier, inc=1, device_id=(mr, on_cols(d)), device_id_type=MESH)
    for d in range(1, nr):
        pl.semaphore_signal(barrier, inc=1, device_id=(on_rows(d), mc), device_id_type=MESH)

    def remote(src, dst, send_sem, recv_sem, device):
        return pltpu.make_async_remote_copy(
            src_ref=src, dst_ref=dst, send_sem=send_sem, recv_sem=recv_sem,
            device_id=device, device_id_type=MESH,
        )

    def owned(index, act):
        if owners == nr:
            act()
        else:
            pl.when(index < owners)(act)

    slab[...] = jnp.zeros_like(slab)

    @pl.loop(0, depths)
    def _(k):
        load_target(k).wait()
        here = span(k, DEPTH)
        th, tl = split(target[here, :])
        high[here, :] = th
        low[here, :] = tl
        load_coupling(k).wait()
        slab[...] += dot3(split(coupling[:, here]), (th, tl), ((1,), (0,)))

    load_source.wait()
    factor_part[...] = lax.dot_general(
        source[...], slab[...], (((0,), (0,)), ((), ())),
        precision=HIGHEST, preferred_element_type=jnp.float32,
    )

    pl.semaphore_wait(barrier, nc - 1 + nr - 1)

    share = R // nc
    small = share // owners
    own_cols = span(mc, share)

    def copy_a(d):
        peer = on_cols(d)
        return remote(
            factor_part.at[span(peer, share), :], from_cols.at[d - 1],
            a_send.at[d - 1], a_recv.at[d - 1], (mr, peer),
        )

    for d in range(1, nc):
        copy_a(d).start()
    for d in range(1, nc):
        copy_a(d).wait_recv()
    part[...] = factor_part[own_cols, :] + tree(jnp.add, [from_cols[d] for d in range(nc - 1)])

    def copy_b(d):
        peer = on_rows(d)
        return peer, remote(
            part.at[span(peer, small), :], from_rows.at[d - 1],
            b_send.at[d - 1], b_recv.at[d - 1], (peer, mc),
        )

    for d in range(1, nr):
        peer, copy = copy_b(d)
        owned(peer, copy.start)

    def own_piece():
        for d in range(1, nr):
            copy_b(d)[1].wait_recv()
        total = part[span(mr, small), :] + tree(jnp.add, [from_rows[d] for d in range(nr - 1)])
        piece[...] = total
        factor[pl.ds(pl.multiple_of(mc * share + mr * small, small), small), :] = total

    owned(mr, own_piece)

    def copy_c(d):
        here = pl.ds(pl.multiple_of(mc * share + mr * small, small), small)
        return remote(
            piece, factor.at[here, :], c_send.at[d - 1], c_recv.at[d - 1], (on_rows(d), mc)
        )

    def spread():
        for d in range(1, nr):
            copy_c(d).start()

    owned(mr, spread)
    for d in range(1, nr):
        owned(lax.rem(mr + nr - d, nr), copy_c(d).wait_recv)

    def copy_d(d):
        return remote(
            factor.at[own_cols, :], factor.at[own_cols, :],
            d_send.at[d - 1], d_recv.at[d - 1], (mr, on_cols(d)),
        )

    for d in range(1, nc):
        copy_d(d).start()
    for d in range(1, nc):
        copy_d(d).wait_recv()

    scaled = factor[...] * (1.0 / math.sqrt(total_rows * total_cols))
    mapped = jnp.dot(
        source[...], scaled, precision=HIGHEST, preferred_element_type=jnp.float32
    ) * (1.0 / R)
    mapped = split(mapped)

    @pl.loop(0, cols // WIDE)
    def _(j):
        here = span(j, WIDE)
        logits[:, here] = dot3(mapped, (high[here, :], low[here, :]), ((1,), (1,)))

    store_logits = pltpu.make_async_copy(logits, logits_hbm, logits_sem)
    store_logits.start()

    colpot_out[...] = jnp.zeros_like(colpot_out)

    def row_copy(sweep, d):
        return remote(
            row_send.at[sweep], row_recv.at[sweep, d - 1],
            rs_send.at[sweep, d - 1], rs_recv.at[sweep, d - 1], (mr, on_cols(d)),
        )

    def col_copy(sweep, d):
        return remote(
            col_send.at[sweep], col_recv.at[sweep, d - 1],
            cs_send.at[sweep, d - 1], cs_recv.at[sweep, d - 1], (on_rows(d), mc),
        )

    def lane(t):
        return slice(t * LANES, (t + 1) * LANES)

    @pl.loop(0, SWEEPS)
    def _(sweep):
        @pl.loop(0, rows // SUB, unroll=4)
        def _(b):
            here = span(b, SUB)
            values = [logits[here, lane(t)] + colpot_out[:, lane(t)] for t in range(tiles)]
            top = tree(jnp.maximum, values)
            row_top[here, :] = top
            row_sum[here, :] = tree(jnp.add, [jnp.exp(value - top) for value in values])

        for c in range(chunks):
            row_send[sweep, c : c + 1, :] = lse_fold(
                row_top[lane(c), :].T, row_sum[lane(c), :].T, 0
            )
        for d in range(1, nc):
            row_copy(sweep, d).start()
        for d in range(1, nc):
            row_copy(sweep, d).wait_recv()
        lse = lse_merge([row_send[sweep]] + [row_recv[sweep, d] for d in range(nc - 1)])
        rowpot = math.log(total_cols) - lse
        for c in range(chunks):
            rowpot_out[lane(c), :] = jnp.broadcast_to(rowpot[c : c + 1, :], (LANES, LANES)).T

        @pl.loop(0, tiles)
        def _(t):
            here = span(t, LANES)
            top = total = None
            for c in range(chunks):
                values = []
                for b in range(blocks):
                    block = slice(c * LANES + b * SUB, c * LANES + (b + 1) * SUB)
                    values.append(logits[block, here] + rowpot_out[block, :])
                peak = tree(jnp.maximum, values if top is None else values + [top])
                fresh = tree(jnp.add, [jnp.exp(value - peak) for value in values])
                total = fresh if top is None else total * jnp.exp(top - peak) + fresh
                top = peak
            col_top[t] = top
            col_sum[t] = total

        for t in range(tiles):
            col_send[sweep, t : t + 1, :] = lse_fold(col_top[t], col_sum[t], 0)
        for d in range(1, nr):
            col_copy(sweep, d).start()
        for d in range(1, nr):
            col_copy(sweep, d).wait_recv()
        lse = lse_merge([col_send[sweep]] + [col_recv[sweep, d] for d in range(nr - 1)])
        colpot = math.log(total_rows) - lse
        for t in range(tiles):
            colpot_out[:, lane(t)] = jnp.broadcast_to(colpot[t : t + 1, :], (SUB, LANES))

    for d in range(1, nc):
        copy_a(d).wait_send()
        copy_d(d).wait_send()
        for sweep in range(SWEEPS):
            row_copy(sweep, d).wait_send()
    for d in range(1, nr):
        peer, copy = copy_b(d)
        owned(peer, copy.wait_send)
        owned(mr, copy_c(d).wait_send)
        for sweep in range(SWEEPS):
            col_copy(sweep, d).wait_send()
    store_logits.wait()


def finish_kernel(logits, rowpot, colpot, out):
    for t in range(logits.shape[1] // LANES):
        here = slice(t * LANES, (t + 1) * LANES)
        out[:, here] = logits[:, here] + rowpot[...] + colpot[0:1, here]


def on_device(nr, nc, coupling, source, target):
    rows, cols = coupling.shape
    share = R // nc
    owners = min(nr, share // SUB)
    small = share // owners
    tiles, chunks = cols // LANES, rows // LANES
    f32 = jnp.float32
    dma = pltpu.SemaphoreType.DMA
    vmem, anywhere = pl.BlockSpec(memory_space=pltpu.VMEM), pl.BlockSpec(memory_space=pl.ANY)
    logits, rowpot, colpot = pl.pallas_call(
        functools.partial(step_kernel, nr, nc, owners),
        out_shape=(
            jax.ShapeDtypeStruct((rows, cols), f32),
            jax.ShapeDtypeStruct((rows, LANES), f32),
            jax.ShapeDtypeStruct((SUB, cols), f32),
        ),
        in_specs=[anywhere] * 3,
        out_specs=(anywhere, vmem, vmem),
        scratch_shapes=[
            pltpu.VMEM((rows, cols), f32),
            pltpu.VMEM((rows, R), f32),
            pltpu.VMEM((cols, R), f32),
            pltpu.VMEM((cols, R), jnp.bfloat16),
            pltpu.VMEM((cols, R), jnp.bfloat16),
            pltpu.VMEM((rows, cols), f32),
            pltpu.VMEM((rows, R), f32),
            pltpu.VMEM((R, R), f32),
            pltpu.VMEM((R, R), f32),
            pltpu.VMEM((nc - 1, share, R), f32),
            pltpu.VMEM((share, R), f32),
            pltpu.VMEM((nr - 1, small, R), f32),
            pltpu.VMEM((small, R), f32),
            pltpu.VMEM((rows, LANES), f32),
            pltpu.VMEM((rows, LANES), f32),
            pltpu.VMEM((tiles, SUB, LANES), f32),
            pltpu.VMEM((tiles, SUB, LANES), f32),
            pltpu.VMEM((SWEEPS, chunks, LANES), f32),
            pltpu.VMEM((SWEEPS, nc - 1, chunks, LANES), f32),
            pltpu.VMEM((SWEEPS, tiles, LANES), f32),
            pltpu.VMEM((SWEEPS, nr - 1, tiles, LANES), f32),
            dma((2, cols // DEPTH + 1)),
            dma,
            dma((nc - 1,)), dma((nc - 1,)),
            dma((nr - 1,)), dma((nr - 1,)),
            dma((nr - 1,)), dma((nr - 1,)),
            dma((nc - 1,)), dma((nc - 1,)),
            dma((SWEEPS, nc - 1)), dma((SWEEPS, nc - 1)),
            dma((SWEEPS, nr - 1)), dma((SWEEPS, nr - 1)),
        ],
        compiler_params=pltpu.CompilerParams(
            collective_id=0, has_side_effects=True, vmem_limit_bytes=40 * 1024 * 1024
        ),
        name="sinkhorn_step",
    )(coupling, source, target)
    height = rows // 8
    return pl.pallas_call(
        finish_kernel,
        out_shape=jax.ShapeDtypeStruct((rows, cols), f32),
        grid=(rows // height,),
        in_specs=[
            pl.BlockSpec((height, cols), lambda i: (i, 0)),
            pl.BlockSpec((height, LANES), lambda i: (i, 0)),
            pl.BlockSpec((SUB, cols), lambda i: (0, 0)),
        ],
        out_specs=pl.BlockSpec((height, cols), lambda i: (i, 0)),
        name="add_potentials",
    )(logits, rowpot, colpot)


def solution(mesh):
    placed = (P("rows", "cols"), P("rows", None), P("cols", None))
    body = functools.partial(on_device, mesh.shape["rows"], mesh.shape["cols"])
    return jax.shard_map(
        body, mesh=mesh, in_specs=placed, out_specs=P("rows", "cols"), check_vma=False
    )
```

time: 325 us -> 74.7 us (0.23)
  blocking collectives: 147 us -> 0 us
  waiting for transfers between devices: 107 us -> 0 us
  Pallas kernels: 0 us -> 66.2 us
  other arithmetic: 35.1 us -> 0 us
  matrix products: 19.2 us -> 0 us
  between operations: 13.5 us -> 0.02 us
  local copies, waits for them, and re-layouts: 1.59 us -> 8.09 us
    psum x2 -> x0, waiting for transfers between devices: 107 us -> none  [the longest x1 71.1 us: on_device(): factor = lax.psum(local_factor, 'rows')]
    pmax x6 -> x0, blocking collectives: 75.8 us -> none  [the longest x3 58.7 us: col_logsumexp(): top = lax.pmax(local_top, 'rows')]
    psum x6 -> x0, blocking collectives: 71.7 us -> none  [the longest x3 52.3 us: col_logsumexp(): total = lax.psum(jnp.sum(jnp.exp(values - top[None, :]), axis=0), 'rows')]
    pallas_call x0 -> x2, Pallas kernels: none -> 66.2 us  [the longest x1 59.5 us: on_device(): pl.pallas_call(functools.partial(step_kernel, nr, nc, owners), out_shape=...]
    dot_general x4 -> x0, matrix products: 19.2 us -> none  [the longest x1 8.48 us: on_device(): lax.dot_general(mapped, target, (((1,), (1,)), ((), ())), precision=highe...]
    reduce_sum x6 -> x0, other arithmetic: 17.8 us -> none  [the longest x3 8.88 us: row_logsumexp(): total = lax.psum(jnp.sum(jnp.exp(values - top[:, None]), axis=1), 'cols')]
    reduce_max x5 -> x0, other arithmetic: 12.7 us -> none  [the longest x3 7.62 us: col_logsumexp(): local_top = jnp.max(values, axis=0)]
    unnamed x4 -> x12, local copies, waits for them, and re-layouts: 1.59 us -> 8.09 us
  transfers between devices with their start and end apart: 2 -> 0, of which waited for: 2 -> 0; matrix products, arithmetic and copies ran while one was open for 0% -> 0% of each run, Pallas kernels for 0% -> 0%
where the time goes in v1:
time: 74.7 us; the launch traced here: 74.3 us
  Pallas kernels  66.2 us (89%)
  local copies, waits for them, and re-layouts  8.09 us (11%)
    pallas_call x1, Pallas kernels, on_device(): pl.pallas_call(functools.partial(step_kernel, nr, nc, owners), out_shape=...  59.5 us
    unnamed x12, local copies, waits for them, and re-layouts  8.09 us
    pallas_call x1, Pallas kernels, on_device(): pl.pallas_call(finish_kernel, out_shape=jax.ShapeDtypeStruct((rows, cols)...  6.67 us

profile of v1, /device:TPU:0, one launch (start us, length us, event | category | flops | bytes accessed | tf_op | source)
XLA Modules:
  0.0 74.3 jit_solution(11283084696432194375)
XLA Ops:
  0.0 0.0 copy-start.1
  0.0 2.2 %copy-done.1 = f32[512,2048]{1,0:T(8,128)S(1)} copy-done((f32[512,2048]{1,0:T(8,128)S(1)}, f32[512,2048]{1,0:T(8,128)}, u32[]{:S(2)}) %copy-start.1) | copy-done | bytes 4194328
  2.2 0.0 copy-start.2
  2.2 1.6 %copy-done.2 = f32[2048,256]{1,0:T(8,128)S(1)} copy-done((f32[2048,256]{1,0:T(8,128)S(1)}, f32[2048,256]{1,0:T(8,128)}, u32[]{:S(2)}) %copy-start.2) | copy-done | bytes 2097176
  3.8 0.0 copy-start.3
  3.8 1.0 %copy-done.3 = f32[512,256]{1,0:T(8,128)S(1)} copy-done((f32[512,256]{1,0:T(8,128)S(1)}, f32[512,256]{1,0:T(8,128)}, u32[]{:S(2)}) %copy-start.3) | copy-done | bytes 524312
  4.8 59.5 %sinkhorn_step.1 = (f32[512,2048]{1,0:T(8,128)S(1)}, f32[512,128]{1,0:T(8,128)S(1)}, f32[8,2048]{1,0:T(8,128)S(1)}) custom-call(f32[512,2048]{1,0:T(8,128)S(1)} %copy-done.1, f32[512,256]{1,0:T(8,128)S(1)} %copy-done.3, f32[2048,256]{1,0:T(8,128)S(1)} %copy-done.2), custom_call_target="tpu_custom_call" | custom-call | tf_op jit(solution)/shard_map/sinkhorn_step/pallas_call | solution.py:304
  64.3 0.0 copy-start
  64.3 1.9 %copy-done = f32[512,2048]{1,0:T(8,128)} copy-done((f32[512,2048]{1,0:T(8,128)}, f32[512,2048]{1,0:T(8,128)S(1)}, u32[]{:S(2)}) %copy-start) | copy-done | bytes 4194328
  66.3 0.0 copy-start.4
  66.3 0.7 copy-done.4
  67.0 0.0 copy-start.5
  67.0 0.6 copy-done.5
  67.6 6.7 %add_potentials.1 = f32[512,2048]{1,0:T(8,128)} custom-call(f32[512,2048]{1,0:T(8,128)} %copy-done, f32[512,128]{1,0:T(8,128)} %copy-done.4, f32[8,2048]{1,0:T(8,128)} %copy-done.5), custom_call_target="tpu_custom_call" | custom-call | tf_op jit(solution)/shard_map/add_potentials/pallas_call | solution.py:350
Async XLA Ops:
  0.0 2.2 %copy-start.1 = (f32[512,2048]{1,0:T(8,128)S(1)}, f32[512,2048]{1,0:T(8,128)}, u32[]{:S(2)}) copy-start(f32[512,2048]{1,0:T(8,128)} %coupling_hbm.1) | copy-start | bytes 12582916
  2.2 1.6 %copy-start.2 = (f32[2048,256]{1,0:T(8,128)S(1)}, f32[2048,256]{1,0:T(8,128)}, u32[]{:S(2)}) copy-start(f32[2048,256]{1,0:T(8,128)} %target_hbm.1) | copy-start | bytes 6291460
  3.8 1.0 %copy-start.3 = (f32[512,256]{1,0:T(8,128)S(1)}, f32[512,256]{1,0:T(8,128)}, u32[]{:S(2)}) copy-start(f32[512,256]{1,0:T(8,128)} %source_hbm.1) | copy-start | bytes 1572868
  64.3 1.9 %copy-start = (f32[512,2048]{1,0:T(8,128)}, f32[512,2048]{1,0:T(8,128)S(1)}, u32[]{:S(2)}) copy-start(f32[512,2048]{1,0:T(8,128)S(1)} %get-tuple-element.8.logits) | copy-start | bytes 12582916
  66.3 0.7 copy-start.4
  67.0 0.6 copy-start.5

commit v2 on v0

v2 whole, which is shorter than its diff:
```python
import functools
import math

import jax
import jax.numpy as jnp
from jax import lax
from jax.experimental import pallas as pl
from jax.experimental.pallas import tpu as pltpu
from jax.sharding import PartitionSpec as P

R = 256
SWEEPS = 3
LANES = 128
SUB = 8
DEPTH = 1024
WIDE = 512
PARTS = 2
STORES = 4
MESH = pl.DeviceIdType.MESH


def tree(op, values):
    while len(values) > 1:
        paired = [op(a, b) for a, b in zip(values[::2], values[1::2])]
        values = paired + values[len(paired) * 2 :]
    return values[0]


def split(x):
    high = x.astype(jnp.bfloat16)
    return high, (x - high.astype(jnp.float32)).astype(jnp.bfloat16)


def dot3(left, right, dims):
    (lh, ll), (rh, rl) = left, right
    dot = functools.partial(
        lax.dot_general, dimension_numbers=(dims, ((), ())), preferred_element_type=jnp.float32
    )
    return dot(lh, rh) + (dot(lh, rl) + dot(ll, rh))


def lse_fold(top, total, axis):
    peak = jnp.max(top, axis=axis, keepdims=True)
    return peak + jnp.log(jnp.sum(total * jnp.exp(top - peak), axis=axis, keepdims=True))


def lse_merge(parts):
    peak = tree(jnp.maximum, parts)
    return peak + jnp.log(tree(jnp.add, [jnp.exp(part - peak) for part in parts]))


def step_kernel(
    nr, nc, owners,
    coupling, source, target,
    logits, rowpot_out, colpot_out,
    high, low, slab, factor_part, factor,
    from_cols, part, from_rows, piece,
    row_top, row_sum, col_top, col_sum,
    row_send, row_recv, col_send, col_recv,
    a_send, a_recv, b_send, b_recv, c_send, c_recv, d_send, d_recv,
    rs_send, rs_recv, cs_send, cs_recv,
):
    rows, cols = logits.shape
    total_rows, total_cols = rows * nr, cols * nc
    mr, mc = lax.axis_index("rows"), lax.axis_index("cols")
    tiles, blocks = cols // LANES, LANES // SUB
    chunks, half = rows // LANES // PARTS, tiles // PARTS

    def span(at, size):
        return pl.ds(pl.multiple_of(at * size, size), size)

    def lane(t):
        return slice(t * LANES, (t + 1) * LANES)

    def on_rows(d):
        return lax.rem(mr + d, nr)

    def on_cols(d):
        return lax.rem(mc + d, nc)

    row_peers = sorted(range(1, nr), key=lambda d: abs(2 * d - nr))
    col_peers = sorted(range(1, nc), key=lambda d: abs(2 * d - nc))

    barrier = pltpu.get_barrier_semaphore()
    for d in col_peers:
        pl.semaphore_signal(barrier, inc=1, device_id=(mr, on_cols(d)), device_id_type=MESH)
    for d in row_peers:
        pl.semaphore_signal(barrier, inc=1, device_id=(on_rows(d), mc), device_id_type=MESH)

    def remote(src, dst, send_sem, recv_sem, device):
        return pltpu.make_async_remote_copy(
            src_ref=src, dst_ref=dst, send_sem=send_sem, recv_sem=recv_sem,
            device_id=device, device_id_type=MESH,
        )

    def owned(index, act):
        if owners == nr:
            act()
        else:
            pl.when(index < owners)(act)

    slab[...] = jnp.zeros_like(slab)

    @pl.loop(0, cols // DEPTH)
    def _(k):
        here = span(k, DEPTH)
        slab[...] += dot3(split(coupling[:, here]), split(target[here, :]), ((1,), (0,)))

    whole = dot3(split(source[...].T), split(slab[...]), ((1,), (0,)))
    for h in range(PARTS):
        factor_part[h] = whole[:, lane(h)]

    pl.semaphore_wait(barrier, nc - 1 + nr - 1)

    share = R // nc
    small = share // owners
    own_cols = span(mc, share)
    own_rows = pl.ds(pl.multiple_of(mc * share + mr * small, small), small)

    def copy_a(h, d):
        peer = on_cols(d)
        return remote(
            factor_part.at[h, span(peer, share), :], from_cols.at[h, d - 1],
            a_send.at[h, d - 1], a_recv.at[h, d - 1], (mr, peer),
        )

    def copy_b(h, d):
        peer = on_rows(d)
        return peer, remote(
            part.at[h, span(peer, small), :], from_rows.at[h, d - 1],
            b_send.at[h, d - 1], b_recv.at[h, d - 1], (peer, mc),
        )

    def copy_c(h, d):
        return remote(
            piece.at[h], factor.at[h, own_rows, :],
            c_send.at[h, d - 1], c_recv.at[h, d - 1], (on_rows(d), mc),
        )

    def copy_d(h, d):
        return remote(
            factor.at[h, own_cols, :], factor.at[h, own_cols, :],
            d_send.at[h, d - 1], d_recv.at[h, d - 1], (mr, on_cols(d)),
        )

    for h in range(PARTS):
        for d in col_peers:
            copy_a(h, d).start()

    @pl.loop(0, cols // WIDE)
    def _(j):
        here = span(j, WIDE)
        high[:, here], low[:, here] = split(target[here, :].T)

    for h in range(PARTS):
        for d in col_peers:
            copy_a(h, d).wait_recv()
        part[h] = factor_part[h, own_cols, :] + tree(
            jnp.add, [from_cols[h, d] for d in range(nc - 1)]
        )
        for d in row_peers:
            peer, copy = copy_b(h, d)
            owned(peer, copy.start)

    for h in range(PARTS):
        def own_piece():
            for d in row_peers:
                copy_b(h, d)[1].wait_recv()
            total = part[h, span(mr, small), :] + tree(
                jnp.add, [from_rows[h, d] for d in range(nr - 1)]
            )
            piece[h] = total
            factor[h, own_rows, :] = total
            for d in row_peers:
                copy_c(h, d).start()

        owned(mr, own_piece)

    for h in range(PARTS):
        for d in row_peers:
            owned(lax.rem(mr + nr - d, nr), copy_c(h, d).wait_recv)
        for d in col_peers:
            copy_d(h, d).start()

    for h in range(PARTS):
        for d in col_peers:
            copy_d(h, d).wait_recv()

    scaled = jnp.concatenate([factor[h] for h in range(PARTS)], axis=1) * (
        1.0 / math.sqrt(total_rows * total_cols)
    )
    mapped = split(dot3(split(source[...]), split(scaled), ((1,), (0,))) * (1.0 / R))

    @pl.loop(0, cols // WIDE)
    def _(j):
        here = span(j, WIDE)
        logits[:, here] = dot3(mapped, (high[:, here], low[:, here]), ((1,), (0,)))

    def row_copy(sweep, g, d):
        return remote(
            row_send.at[sweep, g], row_recv.at[sweep, g, d - 1],
            rs_send.at[sweep, g, d - 1], rs_recv.at[sweep, g, d - 1], (mr, on_cols(d)),
        )

    def col_copy(sweep, h, d):
        return remote(
            col_send.at[sweep, h], col_recv.at[sweep, h, d - 1],
            cs_send.at[sweep, h, d - 1], cs_recv.at[sweep, h, d - 1], (on_rows(d), mc),
        )

    def absorb(values, held):
        top = tree(jnp.maximum, values if held is None else values + [held[0]])
        total = tree(jnp.add, [jnp.exp(value - top) for value in values])
        if held is not None:
            total = total + held[1] * jnp.exp(held[0] - top)
        return top, total

    def row_scan(first, count, seen, fresh, shifted):
        @pl.loop(0, count // SUB, unroll=4)
        def _(b):
            here = pl.ds(pl.multiple_of(first + b * SUB, SUB), SUB)
            values = [logits[here, lane(t)] for t in seen]
            if shifted:
                values = [value + colpot_out[:, lane(t)] for value, t in zip(values, seen)]
            held = None if fresh else (row_top[here, :], row_sum[here, :])
            row_top[here, :], row_sum[here, :] = absorb(values, held)

    def row_share(sweep, g):
        for c in range(chunks):
            here = lane(g * chunks + c)
            row_send[sweep, g, c : c + 1, :] = lse_fold(row_top[here, :].T, row_sum[here, :].T, 0)
        for d in col_peers:
            row_copy(sweep, g, d).start()

    def row_finish(sweep, g):
        for d in col_peers:
            row_copy(sweep, g, d).wait_recv()
        lse = lse_merge([row_send[sweep, g]] + [row_recv[sweep, g, d] for d in range(nc - 1)])
        rowpot = math.log(total_cols) - lse
        for c in range(chunks):
            rowpot_out[lane(g * chunks + c), :] = jnp.broadcast_to(
                rowpot[c : c + 1, :], (LANES, LANES)
            ).T

    def col_scan(g, first, count, fresh):
        @pl.loop(first, first + count)
        def _(t):
            here = span(t, LANES)
            held = None if fresh else (col_top[t], col_sum[t])
            for c in range(g * chunks, (g + 1) * chunks):
                spots = [
                    slice(c * LANES + b * SUB, c * LANES + (b + 1) * SUB) for b in range(blocks)
                ]
                held = absorb([logits[at, here] + rowpot_out[at, :] for at in spots], held)
            col_top[t], col_sum[t] = held

    def col_share(sweep, h):
        for t in range(half):
            at = h * half + t
            col_send[sweep, h, t : t + 1, :] = lse_fold(col_top[at], col_sum[at], 0)
        for d in row_peers:
            col_copy(sweep, h, d).start()

    def col_finish(sweep, h):
        for d in row_peers:
            col_copy(sweep, h, d).wait_recv()
        lse = lse_merge([col_send[sweep, h]] + [col_recv[sweep, h, d] for d in range(nr - 1)])
        colpot = math.log(total_rows) - lse
        for t in range(half):
            colpot_out[:, lane(h * half + t)] = jnp.broadcast_to(colpot[t : t + 1, :], (SUB, LANES))

    height = rows // PARTS
    for sweep in range(SWEEPS):
        if sweep == 0:
            for g in range(PARTS):
                row_scan(g * height, height, range(tiles), True, False)
                row_share(sweep, g)
        else:
            for h in range(PARTS):
                col_finish(sweep - 1, h)
                seen = range(h * half, (h + 1) * half)
                if h < PARTS - 1:
                    row_scan(0, rows, seen, h == 0, True)
            for g in range(PARTS):
                row_scan(g * height, height, seen, False, True)
                row_share(sweep, g)
        for g in range(PARTS - 1):
            row_finish(sweep, g)
            col_scan(g, 0, tiles, g == 0)
        row_finish(sweep, PARTS - 1)
        for h in range(PARTS):
            col_scan(PARTS - 1, h * half, half, False)
            col_share(sweep, h)
    for h in range(PARTS):
        col_finish(SWEEPS - 1, h)

    for h in range(PARTS):
        for d in col_peers:
            copy_a(h, d).wait_send()
            copy_d(h, d).wait_send()
            for sweep in range(SWEEPS):
                row_copy(sweep, h, d).wait_send()
        for d in row_peers:
            peer, copy = copy_b(h, d)
            owned(peer, copy.wait_send)
            owned(mr, copy_c(h, d).wait_send)
            for sweep in range(SWEEPS):
                col_copy(sweep, h, d).wait_send()


def finish_kernel(logits, rowpot, colpot, out, held, sems):
    height = logits.shape[0] // STORES

    def store(i):
        here = slice(i * height, (i + 1) * height)
        return pltpu.make_async_copy(held.at[here, :], out.at[here, :], sems.at[i])

    for i in range(STORES):
        here = slice(i * height, (i + 1) * height)
        for t in range(logits.shape[1] // LANES):
            lane = slice(t * LANES, (t + 1) * LANES)
            held[here, lane] = logits[here, lane] + rowpot[here, :] + colpot[0:1, lane]
        store(i).start()
    for i in range(STORES):
        store(i).wait()


def on_device(nr, nc, coupling, source, target):
    rows, cols = coupling.shape
    share = R // nc
    owners = min(nr, share // SUB)
    small = share // owners
    half, chunks = cols // LANES // PARTS, rows // LANES // PARTS
    tiles = cols // LANES
    f32 = jnp.float32
    dma = pltpu.SemaphoreType.DMA
    vmem, anywhere = pl.BlockSpec(memory_space=pltpu.VMEM), pl.BlockSpec(memory_space=pl.ANY)
    logits, rowpot, colpot = pl.pallas_call(
        functools.partial(step_kernel, nr, nc, owners),
        out_shape=(
            jax.ShapeDtypeStruct((rows, cols), f32),
            jax.ShapeDtypeStruct((rows, LANES), f32),
            jax.ShapeDtypeStruct((SUB, cols), f32),
        ),
        in_specs=[vmem] * 3,
        out_specs=(vmem, vmem, vmem),
        scratch_shapes=[
            pltpu.VMEM((R, cols), jnp.bfloat16),
            pltpu.VMEM((R, cols), jnp.bfloat16),
            pltpu.VMEM((rows, R), f32),
            pltpu.VMEM((PARTS, R, LANES), f32),
            pltpu.VMEM((PARTS, R, LANES), f32),
            pltpu.VMEM((PARTS, nc - 1, share, LANES), f32),
            pltpu.VMEM((PARTS, share, LANES), f32),
            pltpu.VMEM((PARTS, nr - 1, small, LANES), f32),
            pltpu.VMEM((PARTS, small, LANES), f32),
            pltpu.VMEM((rows, LANES), f32),
            pltpu.VMEM((rows, LANES), f32),
            pltpu.VMEM((tiles, SUB, LANES), f32),
            pltpu.VMEM((tiles, SUB, LANES), f32),
            pltpu.VMEM((SWEEPS, PARTS, chunks, LANES), f32),
            pltpu.VMEM((SWEEPS, PARTS, nc - 1, chunks, LANES), f32),
            pltpu.VMEM((SWEEPS, PARTS, half, LANES), f32),
            pltpu.VMEM((SWEEPS, PARTS, nr - 1, half, LANES), f32),
            dma((PARTS, nc - 1)), dma((PARTS, nc - 1)),
            dma((PARTS, nr - 1)), dma((PARTS, nr - 1)),
            dma((PARTS, nr - 1)), dma((PARTS, nr - 1)),
            dma((PARTS, nc - 1)), dma((PARTS, nc - 1)),
            dma((SWEEPS, PARTS, nc - 1)), dma((SWEEPS, PARTS, nc - 1)),
            dma((SWEEPS, PARTS, nr - 1)), dma((SWEEPS, PARTS, nr - 1)),
        ],
        compiler_params=pltpu.CompilerParams(
            collective_id=0, has_side_effects=True, vmem_limit_bytes=36 * 1024 * 1024
        ),
        name="sinkhorn_step",
    )(coupling, source, target)
    return pl.pallas_call(
        finish_kernel,
        out_shape=jax.ShapeDtypeStruct((rows, cols), f32),
        in_specs=[vmem] * 3,
        out_specs=anywhere,
        scratch_shapes=[pltpu.VMEM((rows, cols), f32), dma((STORES,))],
        compiler_params=pltpu.CompilerParams(vmem_limit_bytes=12 * 1024 * 1024),
        name="add_potentials",
    )(logits, rowpot, colpot)


def solution(mesh):
    placed = (P("rows", "cols"), P("rows", None), P("cols", None))
    body = functools.partial(on_device, mesh.shape["rows"], mesh.shape["cols"])
    return jax.shard_map(
        body, mesh=mesh, in_specs=placed, out_specs=P("rows", "cols"), check_vma=False
    )
```

time: 325 us -> 62.7 us (0.19)
  blocking collectives: 147 us -> 0 us
  waiting for transfers between devices: 107 us -> 0 us
  Pallas kernels: 0 us -> 57.7 us
  other arithmetic: 35.1 us -> 0 us
  matrix products: 19.2 us -> 0 us
  between operations: 13.5 us -> 0.01 us
    psum x2 -> x0, waiting for transfers between devices: 107 us -> none  [the longest x1 71.1 us: on_device(): factor = lax.psum(local_factor, 'rows')]
    pmax x6 -> x0, blocking collectives: 75.8 us -> none  [the longest x3 58.7 us: col_logsumexp(): top = lax.pmax(local_top, 'rows')]
    psum x6 -> x0, blocking collectives: 71.7 us -> none  [the longest x3 52.3 us: col_logsumexp(): total = lax.psum(jnp.sum(jnp.exp(values - top[None, :]), axis=0), 'rows')]
    pallas_call x0 -> x2, Pallas kernels: none -> 57.7 us  [the longest x1 55.5 us: on_device(): pl.pallas_call(functools.partial(step_kernel, nr, nc, owners), out_shape=...]
    dot_general x4 -> x0, matrix products: 19.2 us -> none  [the longest x1 8.48 us: on_device(): lax.dot_general(mapped, target, (((1,), (1,)), ((), ())), precision=highe...]
    reduce_sum x6 -> x0, other arithmetic: 17.8 us -> none  [the longest x3 8.88 us: row_logsumexp(): total = lax.psum(jnp.sum(jnp.exp(values - top[:, None]), axis=1), 'cols')]
    reduce_max x5 -> x0, other arithmetic: 12.7 us -> none  [the longest x3 7.62 us: col_logsumexp(): local_top = jnp.max(values, axis=0)]
    add x1 -> x0, other arithmetic: 4.61 us -> none  [on_device(): return logits + rowpot[:, None] + colpot[None, :]]
  transfers between devices with their start and end apart: 2 -> 0, of which waited for: 2 -> 0; matrix products, arithmetic and copies ran while one was open for 0% -> 0% of each run, Pallas kernels for 0% -> 0%
where the time goes in v2:
time: 62.7 us; the launch traced here: 62.5 us
  Pallas kernels  57.7 us (92%)
  local copies, waits for them, and re-layouts  4.82 us (8%)
    pallas_call x1, Pallas kernels, on_device(): pl.pallas_call(functools.partial(step_kernel, nr, nc, owners), out_shape=...  55.5 us
    unnamed x6, local copies, waits for them, and re-layouts  4.82 us
    pallas_call x1, Pallas kernels, on_device(): pl.pallas_call(finish_kernel, out_shape=jax.ShapeDtypeStruct((rows, cols)...  2.16 us

profile of v2, /device:TPU:0, one launch (start us, length us, event | category | flops | bytes accessed | tf_op | source)
XLA Modules:
  0.0 62.5 jit_solution(221455443086190921)
XLA Ops:
  0.0 0.0 copy-start
  0.0 2.2 %copy-done = f32[512,2048]{1,0:T(8,128)S(1)} copy-done((f32[512,2048]{1,0:T(8,128)S(1)}, f32[512,2048]{1,0:T(8,128)}, u32[]{:S(2)}) %copy-start) | copy-done | bytes 4194328
  2.2 0.0 copy-start.1
  2.2 1.6 %copy-done.1 = f32[2048,256]{1,0:T(8,128)S(1)} copy-done((f32[2048,256]{1,0:T(8,128)S(1)}, f32[2048,256]{1,0:T(8,128)}, u32[]{:S(2)}) %copy-start.1) | copy-done | bytes 2097176
  3.8 0.0 copy-start.2
  3.8 1.0 %copy-done.2 = f32[512,256]{1,0:T(8,128)S(1)} copy-done((f32[512,256]{1,0:T(8,128)S(1)}, f32[512,256]{1,0:T(8,128)}, u32[]{:S(2)}) %copy-start.2) | copy-done | bytes 524312
  4.8 55.5 %sinkhorn_step.1 = (f32[512,2048]{1,0:T(8,128)S(1)}, f32[512,128]{1,0:T(8,128)S(1)}, f32[8,2048]{1,0:T(8,128)S(1)}) custom-call(f32[512,2048]{1,0:T(8,128)S(1)} %copy-done, f32[512,256]{1,0:T(8,128)S(1)} %copy-done.2, f32[2048,256]{1,0:T(8,128)S(1)} %copy-done.1), custom_call_target="tpu_custom_call" | custom-call | tf_op jit(solution)/shard_map/sinkhorn_step/pallas_call | solution.py:338
  60.3 2.2 %add_potentials.1 = f32[512,2048]{1,0:T(8,128)} custom-call(f32[512,2048]{1,0:T(8,128)S(1)} %get-tuple-element.8.logits, f32[512,128]{1,0:T(8,128)S(1)} %get-tuple-element.9.rowpot, f32[8,2048]{1,0:T(8,128)S(1)} %get-tuple-element.10.colpot), custom_call_target="tpu_custom_call" | custom-call | tf_op jit(solution)/shard_map/add_potentials/pallas_call | solution.py:377
Async XLA Ops:
  0.0 2.2 %copy-start = (f32[512,2048]{1,0:T(8,128)S(1)}, f32[512,2048]{1,0:T(8,128)}, u32[]{:S(2)}) copy-start(f32[512,2048]{1,0:T(8,128)} %coupling.1) | copy-start | bytes 12582916
  2.2 1.6 %copy-start.1 = (f32[2048,256]{1,0:T(8,128)S(1)}, f32[2048,256]{1,0:T(8,128)}, u32[]{:S(2)}) copy-start(f32[2048,256]{1,0:T(8,128)} %target.1) | copy-start | bytes 6291460
  3.8 1.0 %copy-start.2 = (f32[512,256]{1,0:T(8,128)S(1)}, f32[512,256]{1,0:T(8,128)}, u32[]{:S(2)}) copy-start(f32[512,256]{1,0:T(8,128)} %source.1) | copy-start | bytes 1572868

commit v3 on v2

v3 whole, which is shorter than its diff:
```python
import functools
import math

import jax
import jax.numpy as jnp
from jax import lax
from jax.experimental import pallas as pl
from jax.experimental.pallas import tpu as pltpu
from jax.sharding import PartitionSpec as P

R = 256
SWEEPS = 3
LANES = 128
SUB = 8
LN2 = math.log(2.0)
DEPTH = 512
WIDE = 512
SPLITS = 2
PARTS = 1
STORES = 8
MESH = pl.DeviceIdType.MESH


def tree(op, values):
    while len(values) > 1:
        paired = [op(a, b) for a, b in zip(values[::2], values[1::2])]
        values = paired + values[len(paired) * 2 :]
    return values[0]


def split(x):
    high = x.astype(jnp.bfloat16)
    return high, (x - high.astype(jnp.float32)).astype(jnp.bfloat16)


def beside(x):
    high, low = split(x)
    return jnp.concatenate([high, high, low], axis=1)


def stacked(x):
    high, low = split(x)
    return jnp.concatenate([high, low, high], axis=0)


def dot3(left, right):
    return jnp.dot(left, right, preferred_element_type=jnp.float32)


def lse_fold(top, total, axis):
    peak = jnp.max(top, axis=axis, keepdims=True)
    return peak + jnp.log(jnp.sum(total * jnp.exp2(top - peak), axis=axis, keepdims=True)) * (1.0 / LN2)


def lse_merge(parts):
    peak = tree(jnp.maximum, parts)
    return peak + jnp.log(tree(jnp.add, [jnp.exp2(part - peak) for part in parts])) * (1.0 / LN2)


def step_kernel(
    nr, nc, owners,
    coupling_hbm, source_hbm, target_hbm,
    logits_hbm, rowpot_out, colpot_out,
    coupling, source, target, logits, load_sems, logits_sem,
    spread, slab, factor_part, factor,
    from_cols, part, from_rows, piece,
    row_top, row_sum, col_top, col_sum,
    row_send, row_recv, col_send, col_recv,
    a_send, a_recv, b_send, b_recv, c_send, c_recv, d_send, d_recv,
    rs_send, rs_recv, cs_send, cs_recv,
):
    rows, cols = logits.shape
    total_rows, total_cols = rows * nr, cols * nc
    mr, mc = lax.axis_index("rows"), lax.axis_index("cols")
    tiles, blocks = cols // LANES, LANES // SUB
    chunks, half = rows // LANES // PARTS, tiles // PARTS

    def span(at, size):
        return pl.ds(pl.multiple_of(at * size, size), size)

    def lane(t):
        return slice(t * LANES, (t + 1) * LANES)

    def on_rows(d):
        return lax.rem(mr + d, nr)

    def on_cols(d):
        return lax.rem(mc + d, nc)

    row_peers = sorted(range(1, nr), key=lambda d: -abs(2 * d - nr))
    col_peers = sorted(range(1, nc), key=lambda d: -abs(2 * d - nc))

    def load_target(k):
        return pltpu.make_async_copy(
            target_hbm.at[span(k, DEPTH), :], target.at[span(k, DEPTH), :], load_sems.at[0, k]
        )

    def load_coupling(k):
        return pltpu.make_async_copy(
            coupling_hbm.at[:, span(k, DEPTH)], coupling.at[:, span(k, DEPTH)], load_sems.at[1, k]
        )

    load_source = pltpu.make_async_copy(source_hbm, source, load_sems.at[0, cols // DEPTH])
    for k in range(cols // DEPTH):
        load_target(k).start()
        load_coupling(k).start()
    load_source.start()

    barrier = pltpu.get_barrier_semaphore()
    for d in col_peers:
        pl.semaphore_signal(barrier, inc=1, device_id=(mr, on_cols(d)), device_id_type=MESH)
    for d in row_peers:
        pl.semaphore_signal(barrier, inc=1, device_id=(on_rows(d), mc), device_id_type=MESH)

    def remote(src, dst, send_sem, recv_sem, device):
        return pltpu.make_async_remote_copy(
            src_ref=src, dst_ref=dst, send_sem=send_sem, recv_sem=recv_sem,
            device_id=device, device_id_type=MESH,
        )

    def settle(sized, sem):
        pltpu.make_async_copy(sized, sized, sem).wait()

    def owned(index, act):
        if owners == nr:
            act()
        else:
            pl.when(index < owners)(act)

    slab[...] = jnp.zeros_like(slab)

    @pl.loop(0, cols // DEPTH)
    def _(k):
        here = span(k, DEPTH)
        load_target(k).wait()
        load_coupling(k).wait()
        slab[...] += dot3(beside(coupling[:, here]), stacked(target[here, :]))

    load_source.wait()
    whole = dot3(beside(source[...].T), stacked(slab[...]))
    for h in range(SPLITS):
        factor_part[h] = whole[:, lane(h)]

    pl.semaphore_wait(barrier, nc - 1 + nr - 1)

    share = R // nc
    small = share // owners
    own_cols = span(mc, share)
    own_rows = pl.ds(pl.multiple_of(mc * share + mr * small, small), small)

    def copy_a(h, d):
        peer = on_cols(d)
        return remote(
            factor_part.at[h, span(peer, share), :], from_cols.at[h, d - 1],
            a_send.at[h], a_recv.at[h], (mr, peer),
        )

    def copy_b(h, d):
        peer = on_rows(d)
        return peer, remote(
            part.at[h, span(peer, small), :], from_rows.at[h, d - 1],
            b_send.at[h], b_recv.at[h], (peer, mc),
        )

    def copy_c(h, d):
        return remote(
            piece.at[h], factor.at[h, own_rows, :],
            c_send.at[h], c_recv.at[h], (on_rows(d), mc),
        )

    def copy_d(h, d):
        return remote(
            factor.at[h, own_cols, :], factor.at[h, own_cols, :],
            d_send.at[h], d_recv.at[h], (mr, on_cols(d)),
        )

    for h in range(SPLITS):
        for d in col_peers:
            copy_a(h, d).start()

    @pl.loop(0, cols // WIDE)
    def _(j):
        here = span(j, WIDE)
        spread[:, here] = stacked(target[here, :].T)

    for h in range(SPLITS):
        settle(from_cols.at[h], a_recv.at[h])
        part[h] = factor_part[h, own_cols, :] + tree(
            jnp.add, [from_cols[h, d] for d in range(nc - 1)]
        )
        for d in row_peers:
            peer, copy = copy_b(h, d)
            owned(peer, copy.start)

    for h in range(SPLITS):
        def own_piece():
            settle(from_rows.at[h], b_recv.at[h])
            total = part[h, span(mr, small), :] + tree(
                jnp.add, [from_rows[h, d] for d in range(nr - 1)]
            )
            piece[h] = total
            factor[h, own_rows, :] = total
            for d in row_peers:
                copy_c(h, d).start()

        owned(mr, own_piece)

    for h in range(SPLITS):
        if owners == nr:
            settle(from_rows.at[h], c_recv.at[h])
        else:
            for d in row_peers:
                owned(lax.rem(mr + nr - d, nr), copy_c(h, d).wait_recv)
        for d in col_peers:
            copy_d(h, d).start()

    for h in range(SPLITS):
        settle(from_cols.at[h], d_recv.at[h])

    scaled = jnp.concatenate([factor[h] for h in range(SPLITS)], axis=1) * (
        1.0 / math.sqrt(total_rows * total_cols)
    )
    mapped = beside(dot3(beside(source[...]), stacked(scaled)) * (1.0 / (R * LN2)))

    @pl.loop(0, cols // WIDE)
    def _(j):
        here = span(j, WIDE)
        logits[:, here] = dot3(mapped, spread[:, here])

    store_logits = pltpu.make_async_copy(logits, logits_hbm, logits_sem)
    store_logits.start()

    def row_copy(sweep, g, d):
        return remote(
            row_send.at[sweep, g], row_recv.at[sweep, g, d - 1],
            rs_send.at[sweep, g], rs_recv.at[sweep, g], (mr, on_cols(d)),
        )

    def col_copy(sweep, h, d):
        return remote(
            col_send.at[sweep, h], col_recv.at[sweep, h, d - 1],
            cs_send.at[sweep, h], cs_recv.at[sweep, h], (on_rows(d), mc),
        )

    def absorb(values, held):
        top = tree(jnp.maximum, values if held is None else values + [held[0]])
        total = tree(jnp.add, [jnp.exp2(value - top) for value in values])
        if held is not None:
            total = total + held[1] * jnp.exp2(held[0] - top)
        return top, total

    def row_scan(sweep, count, seen, shifted):
        for c in range(count // LANES):
            tops, sums = [], []
            for b in range(blocks):
                here = slice(c * LANES + b * SUB, c * LANES + (b + 1) * SUB)
                values = [logits[here, lane(t)] for t in seen]
                if shifted:
                    values = [value + colpot_out[:, lane(t)] for value, t in zip(values, seen)]
                top, total = absorb(values, None)
                tops.append(top)
                sums.append(total)
            tops, sums = jnp.concatenate(tops, axis=0).T, jnp.concatenate(sums, axis=0).T
            row_send[sweep, 0, c : c + 1, :] = lse_fold(tops, sums, 0)

    def row_share(sweep, g):
        for d in col_peers:
            row_copy(sweep, g, d).start()

    def row_finish(sweep, g):
        settle(row_recv.at[sweep, g], rs_recv.at[sweep, g])
        lse = lse_merge([row_send[sweep, g]] + [row_recv[sweep, g, d] for d in range(nc - 1)])
        rowpot = math.log2(total_cols) - lse
        for c in range(chunks):
            rowpot_out[lane(g * chunks + c), :] = jnp.broadcast_to(
                rowpot[c : c + 1, :], (LANES, LANES)
            ).T

    def col_scan(g, first, count, fresh):
        @pl.loop(first, first + count, unroll=4)
        def _(t):
            here = span(t, LANES)
            held = None if fresh else (col_top[t], col_sum[t])
            for c in range(g * chunks, (g + 1) * chunks):
                spots = [
                    slice(c * LANES + b * SUB, c * LANES + (b + 1) * SUB) for b in range(blocks)
                ]
                held = absorb([logits[at, here] + rowpot_out[at, :] for at in spots], held)
            col_top[t], col_sum[t] = held

    def col_share(sweep, h):
        for t in range(half):
            at = h * half + t
            col_send[sweep, h, t : t + 1, :] = lse_fold(col_top[at], col_sum[at], 0)
        for d in row_peers:
            col_copy(sweep, h, d).start()

    def col_finish(sweep, h):
        settle(col_recv.at[sweep, h], cs_recv.at[sweep, h])
        lse = lse_merge([col_send[sweep, h]] + [col_recv[sweep, h, d] for d in range(nr - 1)])
        colpot = math.log2(total_rows) - lse
        for t in range(half):
            colpot_out[:, lane(h * half + t)] = jnp.broadcast_to(colpot[t : t + 1, :], (SUB, LANES))

    height = rows // PARTS
    for sweep in range(SWEEPS):
        if sweep == 0:
            for g in range(PARTS):
                row_scan(sweep, height, range(tiles), False)
                row_share(sweep, g)
        else:
            for h in range(PARTS):
                col_finish(sweep - 1, h)
                seen = range(h * half, (h + 1) * half)
            for g in range(PARTS):
                row_scan(sweep, height, seen, True)
                row_share(sweep, g)
        for g in range(PARTS - 1):
            row_finish(sweep, g)
            col_scan(g, 0, tiles, g == 0)
        row_finish(sweep, PARTS - 1)
        for h in range(PARTS):
            col_scan(PARTS - 1, h * half, half, PARTS == 1)
            col_share(sweep, h)
    for h in range(PARTS):
        col_finish(SWEEPS - 1, h)

    for h in range(SPLITS):
        settle(from_cols.at[h], a_send.at[h])
        settle(from_cols.at[h], d_send.at[h])
        if owners == nr:
            settle(from_rows.at[h], b_send.at[h])
        else:
            for d in row_peers:
                peer, copy = copy_b(h, d)
                owned(peer, copy.wait_send)
        owned(mr, lambda: settle(from_rows.at[h], c_send.at[h]))
    for sweep in range(SWEEPS):
        for h in range(PARTS):
            settle(row_recv.at[sweep, h], rs_send.at[sweep, h])
            settle(col_recv.at[sweep, h], cs_send.at[sweep, h])
    store_logits.wait()


def finish_kernel(
    logits_hbm, rowpot_hbm, colpot_hbm, out_hbm, logits, rowpot, colpot, out, load_sems, store_sems
):
    height = logits.shape[0] // STORES

    def band(i):
        return slice(i * height, (i + 1) * height)

    def load(i):
        return pltpu.make_async_copy(
            logits_hbm.at[band(i), :], logits.at[band(i), :], load_sems.at[i]
        )

    def store(i):
        return pltpu.make_async_copy(out.at[band(i), :], out_hbm.at[band(i), :], store_sems.at[i])

    potentials = [
        pltpu.make_async_copy(rowpot_hbm, rowpot, load_sems.at[STORES]),
        pltpu.make_async_copy(colpot_hbm, colpot, load_sems.at[STORES + 1]),
    ]
    for copy in potentials:
        copy.start()
    for i in range(STORES):
        load(i).start()
    for copy in potentials:
        copy.wait()
    for i in range(STORES):
        load(i).wait()
        for t in range(logits.shape[1] // LANES):
            lane = slice(t * LANES, (t + 1) * LANES)
            total = logits[band(i), lane] + rowpot[band(i), :] + colpot[0:1, lane]
            out[band(i), lane] = total * LN2
        store(i).start()
    for i in range(STORES):
        store(i).wait()


def on_device(nr, nc, coupling, source, target):
    rows, cols = coupling.shape
    share = R // nc
    owners = min(nr, share // SUB)
    small = share // owners
    half, chunks = cols // LANES // PARTS, rows // LANES // PARTS
    tiles = cols // LANES
    f32 = jnp.float32
    dma = pltpu.SemaphoreType.DMA
    vmem, anywhere = pl.BlockSpec(memory_space=pltpu.VMEM), pl.BlockSpec(memory_space=pl.ANY)
    logits, rowpot, colpot = pl.pallas_call(
        functools.partial(step_kernel, nr, nc, owners),
        out_shape=(
            jax.ShapeDtypeStruct((rows, cols), f32),
            jax.ShapeDtypeStruct((rows, LANES), f32),
            jax.ShapeDtypeStruct((SUB, cols), f32),
        ),
        in_specs=[anywhere] * 3,
        out_specs=(anywhere, vmem, vmem),
        scratch_shapes=[
            pltpu.VMEM((rows, cols), f32),
            pltpu.VMEM((rows, R), f32),
            pltpu.VMEM((cols, R), f32),
            pltpu.VMEM((rows, cols), f32),
            dma((2, cols // DEPTH + 1)),
            dma,
            pltpu.VMEM((3 * R, cols), jnp.bfloat16),
            pltpu.VMEM((rows, R), f32),
            pltpu.VMEM((SPLITS, R, LANES), f32),
            pltpu.VMEM((SPLITS, R, LANES), f32),
            pltpu.VMEM((SPLITS, nc - 1, share, LANES), f32),
            pltpu.VMEM((SPLITS, share, LANES), f32),
            pltpu.VMEM((SPLITS, nr - 1, small, LANES), f32),
            pltpu.VMEM((SPLITS, small, LANES), f32),
            pltpu.VMEM((rows, LANES), f32),
            pltpu.VMEM((rows, LANES), f32),
            pltpu.VMEM((tiles, SUB, LANES), f32),
            pltpu.VMEM((tiles, SUB, LANES), f32),
            pltpu.VMEM((SWEEPS, PARTS, chunks, LANES), f32),
            pltpu.VMEM((SWEEPS, PARTS, nc - 1, chunks, LANES), f32),
            pltpu.VMEM((SWEEPS, PARTS, half, LANES), f32),
            pltpu.VMEM((SWEEPS, PARTS, nr - 1, half, LANES), f32),
            dma((SPLITS,)), dma((SPLITS,)),
            dma((SPLITS,)), dma((SPLITS,)),
            dma((SPLITS,)), dma((SPLITS,)),
            dma((SPLITS,)), dma((SPLITS,)),
            dma((SWEEPS, PARTS)), dma((SWEEPS, PARTS)),
            dma((SWEEPS, PARTS)), dma((SWEEPS, PARTS)),
        ],
        compiler_params=pltpu.CompilerParams(
            collective_id=0, has_side_effects=True, vmem_limit_bytes=60 * 1024 * 1024
        ),
        name="sinkhorn_step",
    )(coupling, source, target)
    return pl.pallas_call(
        finish_kernel,
        out_shape=jax.ShapeDtypeStruct((rows, cols), f32),
        in_specs=[anywhere] * 3,
        out_specs=anywhere,
        scratch_shapes=[
            pltpu.VMEM((rows, cols), f32),
            pltpu.VMEM((rows, LANES), f32),
            pltpu.VMEM((SUB, cols), f32),
            pltpu.VMEM((rows, cols), f32),
            dma((STORES + 2,)),
            dma((STORES,)),
        ],
        compiler_params=pltpu.CompilerParams(vmem_limit_bytes=60 * 1024 * 1024),
        name="add_potentials",
    )(logits, rowpot, colpot)


def solution(mesh):
    placed = (P("rows", "cols"), P("rows", None), P("cols", None))
    body = functools.partial(on_device, mesh.shape["rows"], mesh.shape["cols"])
    return jax.shard_map(
        body, mesh=mesh, in_specs=placed, out_specs=P("rows", "cols"), check_vma=False
    )
```

time: 62.7 us -> 58.1 us (0.927)
  local copies, waits for them, and re-layouts: 4.82 us -> 0 us
    unnamed x6 -> x0, local copies, waits for them, and re-layouts: 4.82 us -> none
    pallas_call x1, Pallas kernels: 2.16 us -> 3.62 us  [on_device(): pl.pallas_call(finish_kernel, out_shape=jax.ShapeDtypeStruct((rows, cols)...]
    pallas_call x1, Pallas kernels: 55.5 us -> 54.3 us  [on_device(): pl.pallas_call(functools.partial(step_kernel, nr, nc, owners), out_shape=...]
where the time goes in v3:
time: 58.1 us; the launch traced here: 58 us
  Pallas kernels  58 us (100%)
    pallas_call x1, Pallas kernels, on_device(): pl.pallas_call(functools.partial(step_kernel, nr, nc, owners), out_shape=...  54.3 us
    pallas_call x1, Pallas kernels, on_device(): pl.pallas_call(finish_kernel, out_shape=jax.ShapeDtypeStruct((rows, cols)...  3.62 us

profile of v3, /device:TPU:0, one launch (start us, length us, event | category | flops | bytes accessed | tf_op | source)
XLA Modules:
  0.0 58.0 jit_solution(4225345613142324153)
XLA Ops:
  0.0 54.3 %sinkhorn_step.1 = (f32[512,2048]{1,0:T(8,128)}, f32[512,128]{1,0:T(8,128)}, f32[8,2048]{1,0:T(8,128)}) custom-call(f32[512,2048]{1,0:T(8,128)} %coupling_hbm.1, f32[512,256]{1,0:T(8,128)} %source_hbm.1, f32[2048,256]{1,0:T(8,128)} %target_hbm.1), custom_call_target="tpu_custom_call" | custom-call | tf_op jit(solution)/shard_map/sinkhorn_step/pallas_call | solution.py:392
  54.3 3.6 %add_potentials.1 = f32[512,2048]{1,0:T(8,128)} custom-call(f32[512,2048]{1,0:T(8,128)} %get-tuple-element.8.logits_hbm, f32[512,128]{1,0:T(8,128)} %get-tuple-element.9.rowpot_hbm, f32[8,2048]{1,0:T(8,128)} %get-tuple-element.10.colpot_hbm), custom_call_target="tpu_custom_call" | custom-call | tf_op jit(solution)/shard_map/add_potentials/pallas_call | solution.py:436
